TPU v7x, 512 devices: a whole 4x4x16 slice. The times are simulated.
512 devices in a mesh: narrow: 8 (over y, core), wide: 64 (over x, z).
Axes of the slice: x: 4, y: 4, z: 16, core: 2. Of those that a mesh axis runs over, the one named last changes fastest.
Arguments:
- u_real: bfloat16 [1024, 131072], P('narrow', 'wide'), may hold values from -0.01171875 to 0.01171875
- u_imag: bfloat16 [1024, 131072], P('narrow', 'wide'), may hold values from -0.01171875 to 0.01171875
- psi_real: bfloat16 [131072, 512], P('wide', 'narrow'), may hold values from -6 to 6
- psi_imag: bfloat16 [131072, 512], P('wide', 'narrow'), may hold values from -6 to 6
- kick_angle: float32 [512], P('narrow'), may hold values from 0.3 to 2.5
- excited: int32 [131072], P('wide'), may hold values from 0 to 12
Outputs:
- out_real: float32 [512, 1024], P('wide', 'narrow')
- out_imag: float32 [512, 1024], P('wide', 'narrow')
All inputs are finite; a program needn't handle non-finite values.
Results may differ from a plain program's by a relative error of at most 0.0028.
Values may be sent and summed in bfloat16 or wider, within the bound.
A program may use at most 64 MiB of HBM per device.

v0:
```python
import jax
import jax.numpy as jnp
from jax import lax
from jax.sharding import Mesh
from jax.sharding import PartitionSpec as P

NARROW = ("narrow_0", "narrow_1")
WIDE = ("wide_0", "wide_1")


def sent_to_all(array, axis):
    copies = jnp.broadcast_to(array, (lax.axis_size(axis), *array.shape))
    return lax.all_to_all(copies, axis, split_axis=0, concat_axis=0, tiled=True)


def in_order(blocks, dim):
    blocks = jnp.moveaxis(blocks, 0, dim)
    lengths = blocks.shape
    return blocks.reshape(*lengths[:dim], lengths[dim] * lengths[dim + 1], *lengths[dim + 2 :])


def gathered_by_axis(array, axes, dim):
    far, near = axes
    blocks = sent_to_all(sent_to_all(array, far), near)
    return in_order(blocks.swapaxes(0, 1).reshape(-1, *array.shape), dim)


def side_by_side(arrays, axis, dim, along):
    both = jnp.concatenate(arrays, axis=along)
    filled, at, done = (gathered_by_axis(both, axis, dim), 0, [])
    for a in arrays:
        done.append(lax.slice_in_dim(filled, at, at + a.shape[along], axis=along))
        at += a.shape[along]
    return tuple(done)


def cut_along(array, dim, size):
    lengths = array.shape
    blocks = array.reshape(*lengths[:dim], size, lengths[dim] // size, *lengths[dim + 1 :])
    return jnp.moveaxis(blocks, dim, 0)


def summed_on_arrival(array, axis, dim):
    blocks = cut_along(array, dim, lax.axis_size(axis))
    arrived = lax.all_to_all(blocks, axis, split_axis=0, concat_axis=0, tiled=True)
    return arrived.sum(axis=0)


def sum_by_axis(array, axes, dim):
    far, near = axes
    return summed_on_arrival(summed_on_arrival(array, far, dim), near, dim)


def apply_kick(psi_real, psi_imag, kick_angle, excited):
    phases = excited.astype(jnp.float32)[:, None] * kick_angle[None, :]
    cosine = jnp.cos(phases)
    sine = jnp.sin(phases)
    part_real = psi_real.astype(jnp.float32)
    part_imag = psi_imag.astype(jnp.float32)
    kicked_real = (cosine * part_real + sine * part_imag).astype(jnp.bfloat16)
    kicked_imag = (cosine * part_imag - sine * part_real).astype(jnp.bfloat16)
    return (kicked_real, kicked_imag)


def amplitudes(states_real, states_imag, u_real, u_imag):
    contract = (((0,), (1,)), ((), ()))
    rr = lax.dot_general(states_real, u_real, contract, preferred_element_type=jnp.float32)
    ii = lax.dot_general(states_imag, u_imag, contract, preferred_element_type=jnp.float32)
    ri = lax.dot_general(states_imag, u_real, contract, preferred_element_type=jnp.float32)
    ir = lax.dot_general(states_real, u_imag, contract, preferred_element_type=jnp.float32)
    return jnp.concatenate([rr - ii, ri + ir], axis=1)


def on_device(u_real, u_imag, psi_real, psi_imag, kick_angle, excited):
    kicked_real, kicked_imag = apply_kick(psi_real, psi_imag, kick_angle, excited)
    local_rows = u_real.shape[0]
    whole_real, whole_imag = side_by_side(
        (kicked_real, kicked_imag), ("narrow_0", "narrow_1"), 1, 0
    )
    summed = sum_by_axis(
        amplitudes(whole_real, whole_imag, u_real, u_imag), ("wide_0", "wide_1"), 0
    )
    return (summed[:, :local_rows], summed[:, local_rows:])


def solution(mesh):
    split = Mesh(mesh.devices.reshape(4, 2, 4, 16), ("narrow_0", "narrow_1", "wide_0", "wide_1"))
    return jax.shard_map(
        on_device,
        mesh=split,
        in_specs=(
            P(NARROW, WIDE),
            P(NARROW, WIDE),
            P(WIDE, NARROW),
            P(WIDE, NARROW),
            P(NARROW),
            P(WIDE),
        ),
        out_specs=(P(WIDE, NARROW), P(WIDE, NARROW)),
        check_vma=False,
    )
```

profile of v0, /device:TPU:2, one launch (start us, length us, event | category | flops | bytes accessed | tf_op | source)
XLA Modules:
  0.0 90.9 jit_solution(9249566323244092370)
XLA Ops:
  0.6 0.0 copy-start
  0.6 0.8 convert_element_type.15
  1.4 3.5 %fusion.5 = (bf16[2048,64]{0,1:T(8,128)(2,1)S(1)}, bf16[2048,64]{0,1:T(8,128)(2,1)S(1)}) fusion(bf16[2048,64]{0,1:T(8,128)(2,1)} %param.9, bf16[2048,64]{0,1:T(8,128)(2,1)} %param.8, f32[64]{0:T(128)} %param.10, f32[2048]{0:T(1024)S(1)} %convert_element_type.15), kind=kLoop, calls=%fused_computation.9 | loop fusion | flops 1441792 | bytes 1057024 | tf_op jit(solution)/shard_map/convert_element_type | solution.py:60
  5.0 0.2 broadcast_in_dim.8
  5.2 30.6 %all_to_all.20 = bf16[4,4096,64]{1,2,0:T(8,128)(2,1)S(1)} all-to-all(bf16[4,4096,64]{1,2,0:T(8,128)(2,1)S(1)} %broadcast_in_dim.8), channel_id=1, replica_groups=mesh['narrow_0'=4,'narrow_1'=2,'wide_0'=4,'wide_1'=16] {'narrow_0'}, dimensions={0} | all-to-all | bytes 4194304 | tf_op jit(solution)/shard_map/all_to_all | solution.py:13
  35.8 0.5 broadcast_in_dim.9
  36.3 7.1 %all_to_all.21 = bf16[2,4,4096,64]{2,3,1,0:T(8,128)(2,1)S(1)} all-to-all(bf16[2,4,4096,64]{2,3,1,0:T(8,128)(2,1)S(1)} %broadcast_in_dim.9), channel_id=1, replica_groups=mesh['narrow_0'=4,'narrow_1'=2,'wide_0'=4,'wide_1'=16] {'narrow_1'}, dimensions={0} | all-to-all | bytes 8388608 | tf_op jit(solution)/shard_map/all_to_all | solution.py:13
  43.4 0.5 copy.12
  43.9 0.6 fusion.8
  44.5 0.0 copy-done
  44.5 0.9 fusion.11
  45.4 0.0 copy-start.1
  45.4 0.9 fusion.10
  46.3 0.2 copy-done.1
  46.4 0.9 convolution_add_fusion
  47.3 0.9 convolution_subtract_fusion
  48.2 12.9 %all_to_all.22 = f32[4,128,256]{1,2,0:T(8,128)S(1)} all-to-all(f32[4,128,256]{1,2,0:T(8,128)S(1)} %copy_bitcast_fusion), channel_id=1, replica_groups=mesh['narrow_0'=4,'narrow_1'=2,'wide_0'=4,'wide_1'=16] {'wide_0'}, dimensions={0} | all-to-all | bytes 1048576 | tf_op jit(solution)/shard_map/all_to_all | solution.py:45
  61.2 0.1 copy.15
  61.3 29.0 %all_to_all.23 = f32[16,8,256]{2,1,0:T(8,128)S(1)} all-to-all(f32[16,8,256]{2,1,0:T(8,128)S(1)} %bitcast.26), channel_id=1, replica_groups=mesh['narrow_0'=4,'narrow_1'=2,'wide_0'=4,'wide_1'=16] {'wide_1'}, dimensions={0} | all-to-all | bytes 262144 | tf_op jit(solution)/shard_map/all_to_all | solution.py:45
  90.3 0.6 fusion.9
  (4 shorter events, 0.1 us)
Async XLA Ops:
  0.6 43.9 %copy-start = (bf16[128,2048]{1,0:T(8,128)(2,1)S(1)}, bf16[128,2048]{1,0:T(8,128)(2,1)}, u32[]{:S(2)}) copy-start(bf16[128,2048]{1,0:T(8,128)(2,1)} %param.6) | copy-start | bytes 1572868
  45.4 1.0 %copy-start.1 = (bf16[128,2048]{1,0:T(8,128)(2,1)S(1)}, bf16[128,2048]{1,0:T(8,128)(2,1)}, u32[]{:S(2)}) copy-start(bf16[128,2048]{1,0:T(8,128)(2,1)} %param.7) | copy-start | bytes 1572868
where the time goes:
time: 91.3 us; the launch traced here: 90.9 us
  blocking collectives  79.6 us (87%)
  other arithmetic  4.39 us (5%)
  matrix products  3.44 us (4%)
  local copies, waits for them, and re-layouts  2.69 us (3%)
    all_to_all x2, blocking collectives, summed_on_arrival(): lax.all_to_all(blocks, axis, split_axis=0, concat_axis=0, tiled=True)  41.9 us
    all_to_all x2, blocking collectives, sent_to_all(): return lax.all_to_all(copies, axis, split_axis=0, concat_axis=0, tiled=True)  37.7 us
    convert_element_type x1, other arithmetic, apply_kick(): kicked_real = (cosine * part_real + sine * part_imag).astype(jnp.bfloat16)  3.51 us

commit v1 on v0

v1 whole, which is shorter than its diff:
```python
import jax
import jax.numpy as jnp
from jax import lax
from jax.experimental import pallas as pl
from jax.experimental.pallas import tpu as pltpu
from jax.sharding import Mesh
from jax.sharding import PartitionSpec as P

Y, C, X, Z = 4, 2, 4, 16
NARROW = ("y", "c")
WIDE = ("x", "z")
PIECE = 16
PIECES = 4
MESH = pl.DeviceIdType.MESH

OWN, UP, FAR, DOWN = 0, 1, 2, 3
UPWARD = (0, 1, 2, 3)
DOWNWARD = (2, 3, 0, 1)


def kernel(
    angle_hbm,
    excited_hbm,
    psi_real_hbm,
    psi_imag_hbm,
    u_real_hbm,
    u_imag_hbm,
    out_real_ref,
    out_imag_ref,
    angle,
    excited,
    psi,
    w,
    hot,
    table,
    kbuf,
    zsend,
    zbuf,
    xsend,
    xbuf,
    in_sem,
    u_sem,
    u_send,
    u_recv,
    y_send,
    y_recv,
    z_send,
    z_recv,
    x_send,
    x_recv,
):
    y, c, x, z = (lax.axis_index(a) for a in ("y", "c", "x", "z"))
    up, down = lax.rem(y + 1, Y), lax.rem(y + Y - 1, Y)
    half = z // 8
    summing = c == half
    depth = psi.shape[-1]

    barrier = pltpu.get_barrier_semaphore()

    def greet(**where):
        pl.semaphore_signal(barrier, inc=1, device_id=where, device_id_type=MESH)

    greet(y=up)
    greet(y=down)
    greet(c=1 - c)
    for d in range(1, X):
        greet(x=lax.rem(x + d, X), c=half)

    @pl.when(summing)
    def _():
        @pl.loop(1, Z)
        def _(d):
            greet(z=lax.rem(z + d, Z))

    loads = [
        pltpu.make_async_copy(angle_hbm, angle, in_sem.at[0]),
        pltpu.make_async_copy(excited_hbm, excited, in_sem.at[1]),
        pltpu.make_async_copy(psi_real_hbm, psi.at[0], in_sem.at[2]),
        pltpu.make_async_copy(psi_imag_hbm, psi.at[1], in_sem.at[3]),
        pltpu.make_async_copy(u_real_hbm, w.at[c, 0], u_sem.at[0]),
        pltpu.make_async_copy(u_imag_hbm, w.at[c, 1], u_sem.at[1]),
    ]
    for load in loads:
        load.start()

    loads[0].wait()
    number = lax.broadcasted_iota(jnp.int32, (PIECE, 64), 0).astype(jnp.float32)
    phases = number * angle[...]
    full = jnp.concatenate([jnp.cos(phases), jnp.sin(phases)], axis=1)
    high = full.astype(jnp.bfloat16).astype(jnp.float32)
    rest = full - high
    middle = rest.astype(jnp.bfloat16).astype(jnp.float32)
    low = rest - middle
    terms = jnp.concatenate([high, middle, low, jnp.zeros((128 - 3 * PIECE, 128), jnp.float32)], axis=0)
    table[...] = terms.T.astype(jnp.bfloat16)
    loads[1].wait()
    row = lax.broadcasted_iota(jnp.int32, (128, depth), 0) % PIECE
    hot[...] = jnp.where(row == excited[...], 1.0, 0.0).astype(jnp.bfloat16)
    loads[2].wait()
    loads[3].wait()

    def kick(j):
        at = slice(PIECE * j, PIECE * (j + 1))
        angles = jnp.concatenate([table[at, :], table[64 + PIECE * j : 64 + PIECE * (j + 1), :]], axis=0)
        turn = jnp.dot(angles, hot[...], preferred_element_type=jnp.float32)
        cosine, sine = turn[:PIECE], turn[PIECE:]
        real = psi[0, at, :].astype(jnp.float32)
        imag = psi[1, at, :].astype(jnp.float32)
        kbuf[OWN, j, :PIECE] = (cosine * real + sine * imag).astype(jnp.bfloat16)
        kbuf[OWN, j, PIECE:] = (cosine * imag - sine * real).astype(jnp.bfloat16)

    def to_y(source, j, slot, where):
        return pltpu.make_async_remote_copy(
            src_ref=kbuf.at[source, j],
            dst_ref=kbuf.at[slot, j],
            send_sem=y_send,
            recv_sem=y_recv.at[slot, j],
            device_id={"y": where},
            device_id_type=MESH,
        )

    def arrived(slot, j):
        to_y(slot, j, slot, up).wait_recv()

    kick(UPWARD[0])

    @pl.when(summing)
    def _():
        pl.semaphore_wait(barrier, 16)

    @pl.when(jnp.logical_not(summing))
    def _():
        pl.semaphore_wait(barrier, 11)

    to_y(OWN, UPWARD[0], DOWN, up).start()
    kick(DOWNWARD[0])
    to_y(OWN, DOWNWARD[0], UP, down).start()
    u_copies = [
        pltpu.make_async_remote_copy(
            src_ref=u,
            dst_ref=w.at[c, i],
            send_sem=u_send.at[i],
            recv_sem=u_recv.at[i],
            device_id={"c": 1 - c},
            device_id_type=MESH,
        )
        for i, u in enumerate((u_real_hbm, u_imag_hbm))
    ]
    for copy in u_copies:
        copy.start()
    kick(UPWARD[1])
    to_y(OWN, UPWARD[1], DOWN, up).start()
    kick(DOWNWARD[1])
    to_y(OWN, DOWNWARD[1], UP, down).start()
    for t in (2, 3):
        to_y(OWN, UPWARD[t], DOWN, up).start()
        to_y(OWN, DOWNWARD[t], UP, down).start()

    loads[4].wait()
    loads[5].wait()
    for i, u in enumerate((u_real_hbm, u_imag_hbm)):
        pltpu.make_async_remote_copy(
            src_ref=u,
            dst_ref=w.at[1 - c, i],
            send_sem=u_send.at[i],
            recv_sem=u_recv.at[i],
            device_id={"c": 1 - c},
            device_id_type=MESH,
        ).wait_recv()

    def to_z(slot, target):
        j = (target % 8) // 2
        return pltpu.make_async_remote_copy(
            src_ref=zsend.at[slot, j, target % 2],
            dst_ref=zbuf.at[slot, lax.rem(z - target + Z, Z)],
            send_sem=z_send,
            recv_sem=z_recv.at[slot],
            device_id={"z": target},
            device_id_type=MESH,
        )

    def multiply(slot, j):
        products = lax.dot_general(
            kbuf[slot, j],
            w[...].reshape(4 * 128, depth),
            (((1,), (1,)), ((), ())),
            preferred_element_type=jnp.float32,
        )
        by_real, by_imag = products[:PIECE], products[PIECE:]
        parts = []
        for r in range(C):
            at_real, at_imag = slice(256 * r, 256 * r + 128), slice(256 * r + 128, 256 * (r + 1))
            parts.append(
                (by_real[:, at_real] - by_imag[:, at_imag], by_imag[:, at_real] + by_real[:, at_imag])
            )
        for h in range(2):
            at = slice(8 * h, 8 * (h + 1))
            rows = [part[at] for r in range(C) for part in parts[r]]
            zsend[slot, j, h] = jnp.concatenate(rows, axis=0).astype(jnp.bfloat16)
        for h in range(2):
            target = 8 * c + 2 * j + h

            @pl.when(target != z)
            def _():
                to_z(slot, target).start()

    for j in range(PIECES):
        multiply(OWN, j)
    for t in range(PIECES):
        arrived(DOWN, UPWARD[t])
        if t < 2:
            to_y(DOWN, UPWARD[t], FAR, up).start()
        multiply(DOWN, UPWARD[t])
        arrived(UP, DOWNWARD[t])
        if t < 2:
            to_y(UP, DOWNWARD[t], FAR, down).start()
        multiply(UP, DOWNWARD[t])
    for t in range(2):
        arrived(FAR, UPWARD[t])
        multiply(FAR, UPWARD[t])
        arrived(FAR, DOWNWARD[t])
        multiply(FAR, DOWNWARD[t])

    def to_x(slot, r):
        owner = lax.rem(y + slot, Y)
        return owner, pltpu.make_async_remote_copy(
            src_ref=xsend.at[slot, pl.ds(16 * r, 16)],
            dst_ref=xbuf.at[lax.rem(x - owner + X, X)],
            send_sem=x_send,
            recv_sem=x_recv,
            device_id={"x": owner, "c": r},
            device_id_type=MESH,
        )

    @pl.when(summing)
    def _():
        for slot in (OWN, DOWN, UP, FAR):
            others = zbuf.at[slot, pl.ds(1, Z - 1)]
            pltpu.make_async_copy(others, others, z_recv.at[slot]).wait()
            total = zsend[slot, (z % 8) // 2, z % 2].astype(jnp.float32)
            for d in range(1, Z):
                total = total + zbuf[slot, d].astype(jnp.float32)
            xsend[slot] = total
            for r in range(C):
                owner, copy = to_x(slot, r)

                @pl.when(jnp.logical_or(owner != x, c != r))
                def _():
                    copy.start()

    def finish(total):
        out_real_ref[...] = total[:8]
        out_imag_ref[...] = total[8:]

    @pl.when(summing)
    def _():
        others = xbuf.at[pl.ds(1, X - 1)]
        pltpu.make_async_copy(others, others, x_recv).wait()
        mine = xsend[lax.rem(x - y + Y, Y), pl.ds(pl.multiple_of(16 * c, 16), 16)]
        finish(mine + xbuf[1] + xbuf[2] + xbuf[3])

    @pl.when(jnp.logical_not(summing))
    def _():
        pltpu.make_async_copy(xbuf, xbuf, x_recv).wait()
        finish(xbuf[0] + xbuf[1] + xbuf[2] + xbuf[3])

    for copy in u_copies:
        copy.wait_send()
    sent = kbuf.at[pl.ds(0, 3)]
    pltpu.make_async_copy(sent, sent, y_send).wait()

    @pl.when(summing)
    def _():
        for sent, sem in ((zbuf.at[pl.ds(0, 4), pl.ds(0, 7)], z_send), (xsend.at[pl.ds(0, 3)], x_send), (xsend.at[3, pl.ds(0, 16)], x_send)):
            pltpu.make_async_copy(sent, sent, sem).wait()

    @pl.when(jnp.logical_not(summing))
    def _():
        sent = zbuf.at[pl.ds(0, 4), pl.ds(0, 8)]
        pltpu.make_async_copy(sent, sent, z_send).wait()


def on_device(u_real, u_imag, psi_real, psi_imag, kick_angle, excited):
    rows, depth = u_real.shape
    bf16, f32 = jnp.bfloat16, jnp.float32
    any_place = pl.BlockSpec(memory_space=pl.ANY)
    vmem = pl.BlockSpec(memory_space=pltpu.VMEM)
    dma = pltpu.SemaphoreType.DMA
    return pl.pallas_call(
        kernel,
        out_shape=(jax.ShapeDtypeStruct((8, rows), f32),) * 2,
        in_specs=[any_place] * 6,
        out_specs=(vmem, vmem),
        scratch_shapes=[
            pltpu.VMEM((1, 64), f32),
            pltpu.VMEM((1, depth), jnp.int32),
            pltpu.VMEM((2, 64, depth), bf16),
            pltpu.VMEM((C, 2, rows, depth), bf16),
            pltpu.VMEM((128, depth), bf16),
            pltpu.VMEM((128, 128), bf16),
            pltpu.VMEM((Y, PIECES, 2 * PIECE, depth), bf16),
            pltpu.VMEM((Y, PIECES, 2, 32, 128), bf16),
            pltpu.VMEM((Y, Z, 32, 128), bf16),
            pltpu.VMEM((Y, 32, 128), f32),
            pltpu.VMEM((X, 16, 128), f32),
            dma((4,)),
            dma((2,)),
            dma((2,)),
            dma((2,)),
            dma,
            dma((Y, PIECES)),
            dma,
            dma((Y,)),
            dma,
            dma,
        ],
        compiler_params=pltpu.CompilerParams(
            collective_id=0, has_side_effects=True, vmem_limit_bytes=56 << 20
        ),
        cost_estimate=pl.CostEstimate(
            flops=4 * 2 * 256 * 256 * depth, bytes_accessed=6 * rows * depth * 2, transcendentals=0
        ),
    )(kick_angle[None, :], excited[None, :], psi_real.T, psi_imag.T, u_real, u_imag)


def solution(mesh):
    split = Mesh(mesh.devices.reshape(Y, C, X, Z), ("y", "c", "x", "z"))
    return jax.shard_map(
        on_device,
        mesh=split,
        in_specs=(
            P(NARROW, WIDE),
            P(NARROW, WIDE),
            P(WIDE, NARROW),
            P(WIDE, NARROW),
            P(NARROW),
            P(WIDE),
        ),
        out_specs=(P(WIDE, NARROW), P(WIDE, NARROW)),
        check_vma=False,
    )
```

time: 91.3 us -> 44.6 us (0.49)
  the two profiles are of different devices: /device:TPU:2 before, /device:TPU:69 now
where the time goes in v1:
time: 44.6 us; the launch traced here: 44.5 us
  Pallas kernels  42 us (94%)
  local copies, waits for them, and re-layouts  1.86 us (4%)
  between operations  0.65 us (1%)
    pallas_call x1, Pallas kernels, on_device(): pl.pallas_call(kernel, out_shape=(jax.ShapeDtypeStruct((8, rows), f32),)...  42 us
    unnamed x4, local copies, waits for them, and re-layouts  1.86 us

profile of v1, /device:TPU:69, one launch (start us, length us, event | category | flops | bytes accessed | tf_op | source)
XLA Modules:
  0.0 44.5 jit_solution(62494032138615190)
XLA Ops:
  0.6 42.0 %shard_map.77 = (f32[8,128]{1,0:T(8,128)}, f32[8,128]{1,0:T(8,128)}) custom-call(f32[1,64]{1,0:T(1,128)} %bitcast.7, s32[1,2048]{1,0:T(1,128)} %bitcast.6, bf16[64,2048]{1,0:T(8,128)(2,1)} %bitcast.4, bf16[64,2048]{1,0:T(8,128)(2,1)} %bitcast.5, bf16[128,2048]{1,0:T(8,128)(2,1)} %u_real_hbm.1, bf16[128,2048]{1,0:T(8,128)(2,1)} %u_imag_hbm.1), custom_call_target="tpu_custom_call" | custom-call | flops 1073741824 | bytes 3145728 | tf_op jit(solution)/shard_map/pallas_call | solution.py:289
  42.6 0.0 copy-start
  42.6 1.3 %copy.10 = f32[8,128]{1,0:T(8,128)} copy(f32[8,128]{1,0:T(8,128)} %get-tuple-element.4) | data formatting | bytes 8192
  43.9 0.0 copy-done
  43.9 0.6 %copy.11 = f32[8,128]{1,0:T(8,128)} copy(f32[8,128]{1,0:T(8,128)S(1)} %copy-done) | data formatting | bytes 8192
Async XLA Ops:
  42.6 1.3 %copy-start = (f32[8,128]{1,0:T(8,128)S(1)}, f32[8,128]{1,0:T(8,128)}, u32[]{:S(2)}) copy-start(f32[8,128]{1,0:T(8,128)} %get-tuple-element.5) | copy-start | bytes 12292

commit v2 on v1

v2 whole, which is shorter than its diff:
```python
import jax
import jax.numpy as jnp
from jax import lax
from jax.experimental import pallas as pl
from jax.experimental.pallas import tpu as pltpu
from jax.sharding import Mesh
from jax.sharding import PartitionSpec as P

Y, C, X, Z = 4, 2, 4, 16
NARROW = ("y", "c")
WIDE = ("x", "z")
PIECE = 16
PIECES = 4
MESH = pl.DeviceIdType.MESH

OWN, UP, FAR, DOWN = 0, 1, 2, 3
PLACE = {FAR: 0, UP: 1, DOWN: 2}
EARLY = 4
HELLO, RELAY, ACROSS, Y_KNOWN, X_KNOWN, Z_KNOWN = range(6)
PAIRS = ((0, 2, 4, 5), (7, 1, 3, 6))
CORE_OF = tuple(0 if k in PAIRS[0] else 1 for k in range(Z // 2))
NUMBER_OF = tuple(PAIRS[CORE_OF[k]].index(k) for k in range(Z // 2))
KEPT = tuple([(k % 4, p) for p, k in enumerate(PAIRS[c]) if k // 4 == c] for c in range(C))
GIVEN = tuple([(k % 4, p) for p, k in enumerate(PAIRS[1 - c]) if k // 4 == c] for c in range(C))


def kernel(
    angle_hbm,
    excited_hbm,
    psi_real_hbm,
    psi_imag_hbm,
    u_real_hbm,
    u_imag_hbm,
    out_ref,
    angle,
    excited,
    psi,
    w,
    hot,
    table,
    own,
    given,
    kbuf,
    xsend,
    xin,
    zsend,
    zbuf,
    in_sem,
    u_sem,
    u_send,
    u_recv,
    give_send,
    give_recv,
    y_send,
    y_recv,
    x_send,
    x_recv,
    z_send,
    z_recv,
    known,
):
    y, c, x, z = (lax.axis_index(a) for a in ("y", "c", "x", "z"))
    up, down = lax.rem(y + 1, Y), lax.rem(y + Y - 1, Y)
    pair_of_z = z // 2
    core_of_z = sum(jnp.where(pair_of_z == k, CORE_OF[k], 0) for k in range(Z // 2))
    number_of_z = sum(jnp.where(pair_of_z == k, NUMBER_OF[k], 0) for k in range(Z // 2))

    def by_core(values):
        return jnp.where(c == 0, values[0], values[1])

    mine = lax.rem(x - y + Y, Y)
    depth = psi.shape[-1]

    barrier = pltpu.get_barrier_semaphore()

    def greet(**where):
        pl.semaphore_signal(barrier, inc=1, device_id=where, device_id_type=MESH)

    @pl.when(c == 0)
    def _():
        greet(y=up)
        greet(y=down)
        for d in (1, X - 1):
            greet(x=lax.rem(x + d, X))

    @pl.when(c == 1)
    def _():
        greet(c=0)


    loads = [
        pltpu.make_async_copy(angle_hbm, angle, in_sem.at[0]),
        pltpu.make_async_copy(excited_hbm, excited, in_sem.at[1]),
        pltpu.make_async_copy(psi_real_hbm, psi.at[0], in_sem.at[2]),
        pltpu.make_async_copy(psi_imag_hbm, psi.at[1], in_sem.at[3]),
        pltpu.make_async_copy(u_real_hbm, w.at[c, 0], u_sem.at[0]),
        pltpu.make_async_copy(u_imag_hbm, w.at[c, 1], u_sem.at[1]),
    ]
    for load in loads:
        load.start()

    @pl.loop(1, Z)
    def _(d):
        greet(z=lax.rem(z + d, Z), c=1)

    def tell(what, **where):
        pl.semaphore_signal(known.at[what], inc=1, device_id=where, device_id_type=MESH)

    loads[0].wait()
    number = lax.broadcasted_iota(jnp.int32, (PIECE, 64), 0).astype(jnp.float32)
    phases = number * angle[...]
    full = jnp.concatenate([jnp.cos(phases), jnp.sin(phases)], axis=1)
    high = full.astype(jnp.bfloat16).astype(jnp.float32)
    rest = full - high
    middle = rest.astype(jnp.bfloat16).astype(jnp.float32)
    low = rest - middle
    terms = jnp.concatenate([high, middle, low, jnp.zeros((128 - 3 * PIECE, 128), jnp.float32)], axis=0)
    table[...] = terms.T.astype(jnp.bfloat16)
    loads[1].wait()
    row = lax.broadcasted_iota(jnp.int32, (128, depth), 0) % PIECE
    hot[...] = jnp.where(row == excited[...], 1.0, 0.0).astype(jnp.bfloat16)
    loads[2].wait()
    loads[3].wait()

    def kick(place, to):
        at = pl.ds(pl.multiple_of(PIECE * place, PIECE), PIECE)
        sines_at = pl.ds(pl.multiple_of(64 + PIECE * place, PIECE), PIECE)
        angles = jnp.concatenate([table[at, :], table[sines_at, :]], axis=0)
        turn = jnp.dot(angles, hot[...], preferred_element_type=jnp.float32)
        cosine, sine = turn[:PIECE], turn[PIECE:]
        real = psi[0, at, :].astype(jnp.float32)
        imag = psi[1, at, :].astype(jnp.float32)
        to[:PIECE] = (cosine * real + sine * imag).astype(jnp.bfloat16)
        to[PIECE:] = (cosine * imag - sine * real).astype(jnp.bfloat16)

    def keep(i):
        kick(by_core([KEPT[k][i][0] for k in range(C)]), own.at[by_core([KEPT[k][i][1] for k in range(C)])])

    def give(i):
        kick(by_core([GIVEN[k][i][0] for k in range(C)]), given.at[i])
        number = by_core([GIVEN[k][i][1] for k in range(C)])
        pltpu.make_async_remote_copy(
            src_ref=given.at[i],
            dst_ref=own.at[number],
            send_sem=give_send,
            recv_sem=give_recv.at[number],
            device_id={"c": 1 - c},
            device_id_type=MESH,
        ).start()

    def was_given(j):
        for k in range(C):
            if j in [p for _, p in GIVEN[1 - k]]:

                @pl.when(c == k)
                def _():
                    pltpu.make_async_copy(own.at[j], own.at[j], give_recv.at[j]).wait()

    def own_to(j, slot, where):
        return pltpu.make_async_remote_copy(
            src_ref=own.at[j],
            dst_ref=kbuf.at[j, PLACE[slot]],
            send_sem=y_send,
            recv_sem=y_recv.at[slot, j],
            device_id={"y": where},
            device_id_type=MESH,
        )

    def send_own(j):
        own_to(j, DOWN, up).start()
        own_to(j, UP, down).start()

    def pass_on(slot, j):
        part = pl.ds(0, PIECE) if slot == DOWN else pl.ds(PIECE, PIECE)
        pltpu.make_async_remote_copy(
            src_ref=kbuf.at[j, PLACE[slot], part],
            dst_ref=kbuf.at[j, PLACE[FAR], part],
            send_sem=y_send,
            recv_sem=y_recv.at[FAR, j],
            device_id={"y": up if slot == DOWN else down},
            device_id_type=MESH,
        ).start()

    def arrived(slot, j):
        own_to(j, slot, up).wait_recv()

    def pair_arrived(j):
        arrived(DOWN, j)
        pass_on(DOWN, j)
        arrived(UP, j)
        pass_on(UP, j)

    keep(0)
    @pl.when(c == 0)
    def _():
        pl.semaphore_wait(barrier, 5)
        send_own(0)
        tell(HELLO, c=1)
        tell(RELAY, y=up)
        tell(RELAY, y=down)
        for d in (1, X - 1):
            tell(RELAY, x=lax.rem(x + d, X))

    @pl.when(c == 1)
    def _():
        pl.semaphore_wait(known.at[HELLO], 1)

    u_copies = [
        pltpu.make_async_remote_copy(
            src_ref=u,
            dst_ref=w.at[c, i],
            send_sem=u_send.at[i],
            recv_sem=u_recv.at[i],
            device_id={"c": 1 - c},
            device_id_type=MESH,
        )
        for i, u in enumerate((u_real_hbm, u_imag_hbm))
    ]
    give(0)
    give(1)
    for copy in u_copies:
        copy.start()
    keep(1)

    @pl.when(c == 0)
    def _():
        send_own(1)
        pl.semaphore_wait(known.at[RELAY], 4)
        tell(Y_KNOWN, c=1)
        tell(ACROSS, x=lax.rem(x + 2, X))

    @pl.when(c == 1)
    def _():
        pl.semaphore_wait(known.at[Y_KNOWN], 1)
        send_own(0)

    was_given(1)
    pl.when(c == 1)(lambda: send_own(1))
    was_given(2)
    send_own(2)
    pair_arrived(0)
    was_given(3)
    send_own(3)

    loads[4].wait()
    loads[5].wait()
    for i, u in enumerate((u_real_hbm, u_imag_hbm)):
        pltpu.make_async_remote_copy(
            src_ref=u,
            dst_ref=w.at[1 - c, i],
            send_sem=u_send.at[i],
            recv_sem=u_recv.at[i],
            device_id={"c": 1 - c},
            device_id_type=MESH,
        ).wait_recv()

    def multiply(states, pieces):
        products = lax.dot_general(
            states,
            w[...].reshape(4 * 128, depth),
            (((1,), (1,)), ((), ())),
            preferred_element_type=jnp.float32,
        )
        for i, (slot, j) in enumerate(pieces):
            by_real = products[2 * PIECE * i : 2 * PIECE * i + PIECE]
            by_imag = products[2 * PIECE * i + PIECE : 2 * PIECE * (i + 1)]
            parts = []
            for r in range(C):
                at_real, at_imag = slice(256 * r, 256 * r + 128), slice(256 * r + 128, 256 * (r + 1))
                parts.append(by_real[:, at_real] - by_imag[:, at_imag])
                parts.append(by_imag[:, at_real] + by_real[:, at_imag])
            xsend[slot, j] = jnp.concatenate(
                [part[8 * h : 8 * (h + 1)] for h in range(2) for part in parts], axis=0
            ).astype(jnp.bfloat16)

            @pl.when(slot != mine)
            def _():
                owner = lax.rem(y + slot, Y)
                pltpu.make_async_remote_copy(
                    src_ref=xsend.at[slot, j],
                    dst_ref=xin.at[j, lax.rem(x - owner + X, X) - 1],
                    send_sem=x_send,
                    recv_sem=x_recv.at[j],
                    device_id={"x": owner},
                    device_id_type=MESH,
                ).start()

    def sum_over_x(slot, j):
        @pl.when(slot == mine)
        def _():
            pltpu.make_async_copy(xin.at[j], xin.at[j], x_recv.at[j]).wait()
            total = xsend[slot, j].astype(jnp.float32)
            for d in range(X - 1):
                total = total + xin[j, d].astype(jnp.float32)
            zsend[j] = total.astype(jnp.bfloat16)
            for h in range(2):
                target = 2 * by_core([PAIRS[k][j] for k in range(C)]) + h
                for r in range(C):

                    @pl.when(jnp.logical_or(target != z, c != r))
                    def _():
                        pltpu.make_async_remote_copy(
                            src_ref=zsend.at[j, pl.ds(32 * h + 16 * r, 16)],
                            dst_ref=zbuf.at[lax.rem(z - target + Z, Z)],
                            send_sem=z_send,
                            recv_sem=z_recv,
                            device_id={"z": target, "c": r},
                            device_id_type=MESH,
                        ).start()

    def pair(j):
        multiply(kbuf[j, 1:3].reshape(4 * PIECE, depth), [(UP, j), (DOWN, j)])

    def far(j):
        arrived(FAR, j)
        multiply(kbuf[j, 0], [(FAR, j)])

    @pl.when(c == 0)
    def _():
        pl.semaphore_wait(known.at[ACROSS], 1)
        tell(X_KNOWN, c=1)

    @pl.when(c == 1)
    def _():
        pl.semaphore_wait(known.at[X_KNOWN], 1)

    multiply(own[...].reshape(8 * PIECE, depth), [(OWN, j) for j in range(PIECES)])

    pair(0)

    def know_z():
        @pl.when(c == 1)
        def _():
            pl.semaphore_wait(barrier, 2 * (Z - 1))
            tell(Z_KNOWN, c=0)

        @pl.when(c == 0)
        def _():
            pl.semaphore_wait(known.at[Z_KNOWN], 1)

    def sums(*which):
        for slot, j in which:
            sum_over_x(slot, j)

    early = z < EARLY

    def first_sums():
        sums((OWN, 0), (UP, 0), (DOWN, 0), (OWN, 1))

    def second_sums():
        sums((FAR, 0), (UP, 1), (DOWN, 1), (OWN, 2), (OWN, 3))

    pair_arrived(1)
    pair(1)
    far(0)
    pair_arrived(2)

    @pl.when(jnp.logical_not(early))
    def _():
        know_z()
        first_sums()

    pair(2)
    far(1)
    pair_arrived(3)

    @pl.when(jnp.logical_not(early))
    def _():
        second_sums()

    pair(3)

    @pl.when(early)
    def _():
        know_z()
        first_sums()
        second_sums()

    far(2)
    sums((UP, 2), (DOWN, 2), (FAR, 1))
    far(3)
    sums((UP, 3), (DOWN, 3), (FAR, 2), (FAR, 3))

    @pl.when(c == core_of_z)
    def _():
        others = zbuf.at[pl.ds(1, Z - 1)]
        pltpu.make_async_copy(others, others, z_recv).wait()
        here = 32 * (z % 2) + 16 * c
        total = zsend[number_of_z, pl.ds(pl.multiple_of(here, 16), 16)].astype(jnp.float32)
        for d in range(1, Z):
            total = total + zbuf[d].astype(jnp.float32)
        out_ref[...] = total

    @pl.when(c != core_of_z)
    def _():
        pltpu.make_async_copy(zbuf, zbuf, z_recv).wait()
        total = zbuf[0].astype(jnp.float32)
        for d in range(1, Z):
            total = total + zbuf[d].astype(jnp.float32)
        out_ref[...] = total

    for copy in u_copies:
        copy.wait_send()
    pltpu.make_async_copy(given, given, give_send).wait()
    pltpu.make_async_copy(kbuf, kbuf, y_send).wait()
    pltpu.make_async_copy(xin, xin, x_send).wait()

    @pl.when(c == core_of_z)
    def _():
        sent = zbuf.at[pl.ds(1, Z - 1)]
        pltpu.make_async_copy(sent, sent, z_send).wait()

    @pl.when(c != core_of_z)
    def _():
        pltpu.make_async_copy(zbuf, zbuf, z_send).wait()


def on_device(u_real, u_imag, psi_real, psi_imag, kick_angle, excited):
    rows, depth = u_real.shape
    bf16, f32 = jnp.bfloat16, jnp.float32
    any_place = pl.BlockSpec(memory_space=pl.ANY)
    vmem = pl.BlockSpec(memory_space=pltpu.VMEM)
    dma = pltpu.SemaphoreType.DMA
    out = pl.pallas_call(
        kernel,
        out_shape=jax.ShapeDtypeStruct((16, rows), f32),
        in_specs=[any_place] * 6,
        out_specs=vmem,
        scratch_shapes=[
            pltpu.VMEM((1, 64), f32),
            pltpu.VMEM((1, depth), jnp.int32),
            pltpu.VMEM((2, 64, depth), bf16),
            pltpu.VMEM((C, 2, rows, depth), bf16),
            pltpu.VMEM((128, depth), bf16),
            pltpu.VMEM((128, 128), bf16),
            pltpu.VMEM((PIECES, 2 * PIECE, depth), bf16),
            pltpu.VMEM((2, 2 * PIECE, depth), bf16),
            pltpu.VMEM((PIECES, 3, 2 * PIECE, depth), bf16),
            pltpu.VMEM((Y, PIECES, 64, rows), bf16),
            pltpu.VMEM((PIECES, X - 1, 64, rows), bf16),
            pltpu.VMEM((PIECES, 64, rows), bf16),
            pltpu.VMEM((Z, 16, rows), bf16),
            dma((4,)),
            dma((2,)),
            dma((2,)),
            dma((2,)),
            dma,
            dma((PIECES,)),
            dma,
            dma((Y, PIECES)),
            dma,
            dma((PIECES,)),
            dma,
            dma,
            pltpu.SemaphoreType.REGULAR((6,)),
        ],
        compiler_params=pltpu.CompilerParams(
            collective_id=0, has_side_effects=True, vmem_limit_bytes=56 << 20
        ),
        cost_estimate=pl.CostEstimate(
            flops=4 * 2 * 256 * 256 * depth, bytes_accessed=6 * rows * depth * 2, transcendentals=0
        ),
    )(kick_angle[None, :], excited[None, :], psi_real.T, psi_imag.T, u_real, u_imag)
    return out[:8], out[8:]


def solution(mesh):
    split = Mesh(mesh.devices.reshape(Y, C, X, Z), ("y", "c", "x", "z"))
    return jax.shard_map(
        on_device,
        mesh=split,
        in_specs=(
            P(NARROW, WIDE),
            P(NARROW, WIDE),
            P(WIDE, NARROW),
            P(WIDE, NARROW),
            P(NARROW),
            P(WIDE),
        ),
        out_specs=(P(WIDE, NARROW), P(WIDE, NARROW)),
        check_vma=False,
    )
```

time: 44.6 us -> 41.6 us (0.933)
  Pallas kernels: 42 us -> 39.5 us
  local copies, waits for them, and re-layouts: 1.86 us -> 1.28 us
    pallas_call x1, Pallas kernels: 42 us -> 39.5 us  [on_device(): pl.pallas_call(kernel, out_shape=jax.ShapeDtypeStruct((16, rows), f32), i...]
    unnamed x4 -> x0, local copies, waits for them, and re-layouts: 1.86 us -> none
    slice x0 -> x1, local copies, waits for them, and re-layouts: none -> 1.28 us  [on_device(): return (out[:8], out[8:])]
where the time goes in v2:
time: 41.6 us; the launch traced here: 41.4 us
  Pallas kernels  39.5 us (95%)
  local copies, waits for them, and re-layouts  1.28 us (3%)
  between operations  0.64 us (2%)
    pallas_call x1, Pallas kernels, on_device(): pl.pallas_call(kernel, out_shape=jax.ShapeDtypeStruct((16, rows), f32), i...  39.5 us
    slice x1, local copies, waits for them, and re-layouts, on_device(): return (out[:8], out[8:])  1.28 us

profile of v2, /device:TPU:69, one launch (start us, length us, event | category | flops | bytes accessed | tf_op | source)
XLA Modules:
  0.0 41.4 jit_solution(12599210290379644691)
XLA Ops:
  0.6 39.5 %shard_map.77 = f32[16,128]{1,0:T(8,128)} custom-call(f32[1,64]{1,0:T(1,128)} %bitcast.7, s32[1,2048]{1,0:T(1,128)} %bitcast.6, bf16[64,2048]{1,0:T(8,128)(2,1)} %bitcast.4, bf16[64,2048]{1,0:T(8,128)(2,1)} %bitcast.5, bf16[128,2048]{1,0:T(8,128)(2,1)} %u_real_hbm.1, bf16[128,2048]{1,0:T(8,128)(2,1)} %u_imag_hbm.1), custom_call_target="tpu_custom_call" | custom-call | flops 1073741824 | bytes 3145728 | tf_op jit(solution)/shard_map/pallas_call | solution.py:424
  40.2 1.3 %fusion = (f32[8,128]{1,0:T(8,128)}, f32[8,128]{1,0:T(8,128)}) fusion(f32[16,128]{1,0:T(8,128)} %shard_map.77), kind=kLoop, calls=%fused_computation | loop fusion | bytes 16384 | tf_op jit(solution)/shard_map/slice | solution.py:464

commit v3 on v2

--- a/solution.py
+++ b/solution.py
@@ -17,7 +17,7 @@
 PLACE = {FAR: 0, UP: 1, DOWN: 2}
 EARLY = 4
 HELLO, RELAY, ACROSS, Y_KNOWN, X_KNOWN, Z_KNOWN = range(6)
-PAIRS = ((0, 2, 4, 5), (7, 1, 3, 6))
+PAIRS = ((0, 2, 4, 5), (1, 3, 7, 6))
 CORE_OF = tuple(0 if k in PAIRS[0] else 1 for k in range(Z // 2))
 NUMBER_OF = tuple(PAIRS[CORE_OF[k]].index(k) for k in range(Z // 2))
 KEPT = tuple([(k % 4, p) for p, k in enumerate(PAIRS[c]) if k // 4 == c] for c in range(C))
@@ -232,15 +232,15 @@
     @pl.when(c == 1)
     def _():
         pl.semaphore_wait(known.at[Y_KNOWN], 1)
-        send_own(0)
-
+
+    was_given(0)
+    pl.when(c == 1)(lambda: send_own(0))
     was_given(1)
     pl.when(c == 1)(lambda: send_own(1))
     was_given(2)
+    pair_arrived(0)
     send_own(2)
-    pair_arrived(0)
     was_given(3)
-    send_own(3)
 
     loads[4].wait()
     loads[5].wait()
@@ -345,20 +345,29 @@
     early = z < EARLY
 
     def first_sums():
-        sums((OWN, 0), (UP, 0), (DOWN, 0), (OWN, 1))
+        sums((OWN, 0), (UP, 0), (DOWN, 0))
 
     def second_sums():
-        sums((FAR, 0), (UP, 1), (DOWN, 1), (OWN, 2), (OWN, 3))
+        sums((FAR, 0))
+
+    def third_sums():
+        sums((OWN, 1), (UP, 1), (DOWN, 1), (OWN, 2), (OWN, 3))
 
     pair_arrived(1)
+    send_own(3)
+    far(0)
     pair(1)
-    far(0)
-    pair_arrived(2)
 
     @pl.when(jnp.logical_not(early))
     def _():
         know_z()
         first_sums()
+
+    pair_arrived(2)
+
+    @pl.when(jnp.logical_not(early))
+    def _():
+        second_sums()
 
     pair(2)
     far(1)
@@ -366,7 +375,7 @@
 
     @pl.when(jnp.logical_not(early))
     def _():
-        second_sums()
+        third_sums()
 
     pair(3)
 
@@ -375,11 +384,27 @@
         know_z()
         first_sums()
         second_sums()
+        third_sums()
 
     far(2)
     sums((UP, 2), (DOWN, 2), (FAR, 1))
     far(3)
     sums((UP, 3), (DOWN, 3), (FAR, 2), (FAR, 3))
+
+    for copy in u_copies:
+        copy.wait_send()
+    pltpu.make_async_copy(given, given, give_send).wait()
+    pltpu.make_async_copy(kbuf, kbuf, y_send).wait()
+    pltpu.make_async_copy(xin, xin, x_send).wait()
+
+    @pl.when(c == core_of_z)
+    def _():
+        sent = zbuf.at[pl.ds(1, Z - 1)]
+        pltpu.make_async_copy(sent, sent, z_send).wait()
+
+    @pl.when(c != core_of_z)
+    def _():
+        pltpu.make_async_copy(zbuf, zbuf, z_send).wait()
 
     @pl.when(c == core_of_z)
     def _():
@@ -398,21 +423,6 @@
         for d in range(1, Z):
             total = total + zbuf[d].astype(jnp.float32)
         out_ref[...] = total
-
-    for copy in u_copies:
-        copy.wait_send()
-    pltpu.make_async_copy(given, given, give_send).wait()
-    pltpu.make_async_copy(kbuf, kbuf, y_send).wait()
-    pltpu.make_async_copy(xin, xin, x_send).wait()
-
-    @pl.when(c == core_of_z)
-    def _():
-        sent = zbuf.at[pl.ds(1, Z - 1)]
-        pltpu.make_async_copy(sent, sent, z_send).wait()
-
-    @pl.when(c != core_of_z)
-    def _():
-        pltpu.make_async_copy(zbuf, zbuf, z_send).wait()
 
 
 def on_device(u_real, u_imag, psi_real, psi_imag, kick_angle, excited):
@@ -423,7 +433,7 @@
     dma = pltpu.SemaphoreType.DMA
     out = pl.pallas_call(
         kernel,
-        out_shape=jax.ShapeDtypeStruct((16, rows), f32),
+        out_shape=pltpu.VMEM((16, rows), f32),
         in_specs=[any_place] * 6,
         out_specs=vmem,
         scratch_shapes=[

time: 41.6 us -> 36.4 us (0.87)
  the two profiles are of different devices: /device:TPU:69 before, /device:TPU:1 now
where the time goes in v3:
time: 36.4 us; the launch traced here: 36.2 us
  Pallas kernels  35 us (96%)
  between operations  0.64 us (2%)
  local copies, waits for them, and re-layouts  0.6 us (2%)
    pallas_call x1, Pallas kernels, on_device(): pl.pallas_call(kernel, out_shape=pltpu.VMEM((16, rows), f32), in_specs=[a...  35 us

profile of v3, /device:TPU:1, one launch (start us, length us, event | category | flops | bytes accessed | tf_op | source)
XLA Modules:
  0.0 36.2 jit_solution(7813682775434243117)
XLA Ops:
  0.6 35.0 %shard_map.77 = f32[16,128]{1,0:T(8,128)S(1)} custom-call(f32[1,64]{1,0:T(1,128)} %bitcast.7, s32[1,2048]{1,0:T(1,128)} %bitcast.6, bf16[64,2048]{1,0:T(8,128)(2,1)} %bitcast.4, bf16[64,2048]{1,0:T(8,128)(2,1)} %bitcast.5, bf16[128,2048]{1,0:T(8,128)(2,1)} %u_real_hbm.1, bf16[128,2048]{1,0:T(8,128)(2,1)} %u_imag_hbm.1), custom_call_target="tpu_custom_call" | custom-call | flops 1073741824 | bytes 3145728 | tf_op jit(solution)/shard_map/pallas_call | solution.py:434
  35.6 0.6 %fusion = (f32[8,128]{1,0:T(8,128)}, f32[8,128]{1,0:T(8,128)}) fusion(f32[16,128]{1,0:T(8,128)S(1)} %shard_map.77), kind=kLoop, calls=%fused_computation | loop fusion | bytes 16384 | tf_op jit(solution)/shard_map/slice | solution.py:474

commit v4 on v3

--- a/solution.py
+++ b/solution.py
@@ -16,8 +16,8 @@
 OWN, UP, FAR, DOWN = 0, 1, 2, 3
 PLACE = {FAR: 0, UP: 1, DOWN: 2}
 EARLY = 4
-HELLO, RELAY, ACROSS, Y_KNOWN, X_KNOWN, Z_KNOWN = range(6)
-PAIRS = ((0, 2, 4, 5), (1, 3, 7, 6))
+RELAY, Y_KNOWN, X_KNOWN, Z_KNOWN = range(4)
+PAIRS = ((0, 2, 7, 5), (1, 3, 6, 4))
 CORE_OF = tuple(0 if k in PAIRS[0] else 1 for k in range(Z // 2))
 NUMBER_OF = tuple(PAIRS[CORE_OF[k]].index(k) for k in range(Z // 2))
 KEPT = tuple([(k % 4, p) for p, k in enumerate(PAIRS[c]) if k // 4 == c] for c in range(C))
@@ -76,16 +76,15 @@
     def greet(**where):
         pl.semaphore_signal(barrier, inc=1, device_id=where, device_id_type=MESH)
 
-    @pl.when(c == 0)
-    def _():
-        greet(y=up)
-        greet(y=down)
-        for d in (1, X - 1):
-            greet(x=lax.rem(x + d, X))
+    greet(y=up, c=0)
+    greet(y=down, c=0)
 
     @pl.when(c == 1)
     def _():
         greet(c=0)
+
+    for d in (1, X - 1):
+        greet(x=lax.rem(x + d, X), c=0)
 
 
     loads = [
@@ -98,10 +97,6 @@
     ]
     for load in loads:
         load.start()
-
-    @pl.loop(1, Z)
-    def _(d):
-        greet(z=lax.rem(z + d, Z), c=1)
 
     def tell(what, **where):
         pl.semaphore_signal(known.at[what], inc=1, device_id=where, device_id_type=MESH)
@@ -191,19 +186,18 @@
         pass_on(UP, j)
 
     keep(0)
+
     @pl.when(c == 0)
     def _():
-        pl.semaphore_wait(barrier, 5)
+        pl.semaphore_wait(barrier, 9)
+        tell(Y_KNOWN, c=1)
         send_own(0)
-        tell(HELLO, c=1)
-        tell(RELAY, y=up)
-        tell(RELAY, y=down)
         for d in (1, X - 1):
             tell(RELAY, x=lax.rem(x + d, X))
 
     @pl.when(c == 1)
     def _():
-        pl.semaphore_wait(known.at[HELLO], 1)
+        pl.semaphore_wait(known.at[Y_KNOWN], 1)
 
     u_copies = [
         pltpu.make_async_remote_copy(
@@ -216,6 +210,10 @@
         )
         for i, u in enumerate((u_real_hbm, u_imag_hbm))
     ]
+    @pl.loop(1, Z)
+    def _(d):
+        greet(z=lax.rem(z + d, Z), c=1)
+
     give(0)
     give(1)
     for copy in u_copies:
@@ -225,13 +223,6 @@
     @pl.when(c == 0)
     def _():
         send_own(1)
-        pl.semaphore_wait(known.at[RELAY], 4)
-        tell(Y_KNOWN, c=1)
-        tell(ACROSS, x=lax.rem(x + 2, X))
-
-    @pl.when(c == 1)
-    def _():
-        pl.semaphore_wait(known.at[Y_KNOWN], 1)
 
     was_given(0)
     pl.when(c == 1)(lambda: send_own(0))
@@ -317,7 +308,7 @@
 
     @pl.when(c == 0)
     def _():
-        pl.semaphore_wait(known.at[ACROSS], 1)
+        pl.semaphore_wait(known.at[RELAY], 2)
         tell(X_KNOWN, c=1)
 
     @pl.when(c == 1)
@@ -462,7 +453,7 @@
             dma((PIECES,)),
             dma,
             dma,
-            pltpu.SemaphoreType.REGULAR((6,)),
+            pltpu.SemaphoreType.REGULAR((4,)),
         ],
         compiler_params=pltpu.CompilerParams(
             collective_id=0, has_side_effects=True, vmem_limit_bytes=56 << 20

time: 36.4 us -> 35.9 us (0.986)
  Pallas kernels: 35 us -> 34.5 us
    pallas_call x1, Pallas kernels: 35 us -> 34.5 us  [on_device(): pl.pallas_call(kernel, out_shape=pltpu.VMEM((16, rows), f32), in_specs=[a...]
where the time goes in v4:
time: 35.9 us; the launch traced here: 35.7 us
  Pallas kernels  34.5 us (96%)
  between operations  0.64 us (2%)
  local copies, waits for them, and re-layouts  0.6 us (2%)
    pallas_call x1, Pallas kernels, on_device(): pl.pallas_call(kernel, out_shape=pltpu.VMEM((16, rows), f32), in_specs=[a...  34.5 us

profile of v4, /device:TPU:1, one launch (start us, length us, event | category | flops | bytes accessed | tf_op | source)
XLA Modules:
  0.0 35.7 jit_solution(18311788242788646075)
XLA Ops:
  0.6 34.5 %shard_map.77 = f32[16,128]{1,0:T(8,128)S(1)} custom-call(f32[1,64]{1,0:T(1,128)} %bitcast.7, s32[1,2048]{1,0:T(1,128)} %bitcast.6, bf16[64,2048]{1,0:T(8,128)(2,1)} %bitcast.4, bf16[64,2048]{1,0:T(8,128)(2,1)} %bitcast.5, bf16[128,2048]{1,0:T(8,128)(2,1)} %u_real_hbm.1, bf16[128,2048]{1,0:T(8,128)(2,1)} %u_imag_hbm.1), custom_call_target="tpu_custom_call" | custom-call | flops 1073741824 | bytes 3145728 | tf_op jit(solution)/shard_map/pallas_call | solution.py:425
  35.1 0.6 %fusion = (f32[8,128]{1,0:T(8,128)}, f32[8,128]{1,0:T(8,128)}) fusion(f32[16,128]{1,0:T(8,128)S(1)} %shard_map.77), kind=kLoop, calls=%fused_computation | loop fusion | bytes 16384 | tf_op jit(solution)/shard_map/slice | solution.py:465

commit v5 on v4

--- a/solution.py
+++ b/solution.py
@@ -319,11 +319,16 @@
 
     pair(0)
 
+    def hear_z():
+        pl.semaphore_wait(barrier, 2 * (Z - 1))
+        tell(Z_KNOWN, c=0)
+
+    pl.when(jnp.logical_and(c == 1, z >= 8))(hear_z)
+
     def know_z():
-        @pl.when(c == 1)
+        @pl.when(jnp.logical_and(c == 1, z < 8))
         def _():
-            pl.semaphore_wait(barrier, 2 * (Z - 1))
-            tell(Z_KNOWN, c=0)
+            hear_z()
 
         @pl.when(c == 0)
         def _():

time: 35.9 us -> 35.2 us (0.981)
  the two profiles are of different devices: /device:TPU:1 before, /device:TPU:485 now
where the time goes in v5:
time: 35.2 us; the launch traced here: 35 us
  Pallas kernels  33.8 us (96%)
  between operations  0.64 us (2%)
  local copies, waits for them, and re-layouts  0.6 us (2%)
    pallas_call x1, Pallas kernels, on_device(): pl.pallas_call(kernel, out_shape=pltpu.VMEM((16, rows), f32), in_specs=[a...  33.8 us

profile of v5, /device:TPU:485, one launch (start us, length us, event | category | flops | bytes accessed | tf_op | source)
XLA Modules:
  0.0 35.0 jit_solution(13883530057398485479)
XLA Ops:
  0.6 33.8 %shard_map.77 = f32[16,128]{1,0:T(8,128)S(1)} custom-call(f32[1,64]{1,0:T(1,128)} %bitcast.7, s32[1,2048]{1,0:T(1,128)} %bitcast.6, bf16[64,2048]{1,0:T(8,128)(2,1)} %bitcast.4, bf16[64,2048]{1,0:T(8,128)(2,1)} %bitcast.5, bf16[128,2048]{1,0:T(8,128)(2,1)} %u_real_hbm.1, bf16[128,2048]{1,0:T(8,128)(2,1)} %u_imag_hbm.1), custom_call_target="tpu_custom_call" | custom-call | flops 1073741824 | bytes 3145728 | tf_op jit(solution)/shard_map/pallas_call | solution.py:430
  34.4 0.6 %fusion = (f32[8,128]{1,0:T(8,128)}, f32[8,128]{1,0:T(8,128)}) fusion(f32[16,128]{1,0:T(8,128)S(1)} %shard_map.77), kind=kLoop, calls=%fused_computation | loop fusion | bytes 16384 | tf_op jit(solution)/shard_map/slice | solution.py:470

commit v6 on v5

--- a/solution.py
+++ b/solution.py
@@ -17,7 +17,7 @@
 PLACE = {FAR: 0, UP: 1, DOWN: 2}
 EARLY = 4
 RELAY, Y_KNOWN, X_KNOWN, Z_KNOWN = range(4)
-PAIRS = ((0, 2, 7, 5), (1, 3, 6, 4))
+PAIRS = ((0, 2, 6, 5), (1, 7, 3, 4))
 CORE_OF = tuple(0 if k in PAIRS[0] else 1 for k in range(Z // 2))
 NUMBER_OF = tuple(PAIRS[CORE_OF[k]].index(k) for k in range(Z // 2))
 KEPT = tuple([(k % 4, p) for p, k in enumerate(PAIRS[c]) if k // 4 == c] for c in range(C))

time: 35.2 us -> 36.4 us (1.034)
  the two profiles are of different devices: /device:TPU:485 before, /device:TPU:197 now
where the time goes in v6:
time: 36.4 us; the launch traced here: 36.2 us
  Pallas kernels  35 us (96%)
  between operations  0.64 us (2%)
  local copies, waits for them, and re-layouts  0.6 us (2%)
    pallas_call x1, Pallas kernels, on_device(): pl.pallas_call(kernel, out_shape=pltpu.VMEM((16, rows), f32), in_specs=[a...  35 us

profile of v6, /device:TPU:197, one launch (start us, length us, event | category | flops | bytes accessed | tf_op | source)
XLA Modules:
  0.0 36.2 jit_solution(6614934712686537386)
XLA Ops:
  0.6 35.0 %shard_map.77 = f32[16,128]{1,0:T(8,128)S(1)} custom-call(f32[1,64]{1,0:T(1,128)} %bitcast.7, s32[1,2048]{1,0:T(1,128)} %bitcast.6, bf16[64,2048]{1,0:T(8,128)(2,1)} %bitcast.4, bf16[64,2048]{1,0:T(8,128)(2,1)} %bitcast.5, bf16[128,2048]{1,0:T(8,128)(2,1)} %u_real_hbm.1, bf16[128,2048]{1,0:T(8,128)(2,1)} %u_imag_hbm.1), custom_call_target="tpu_custom_call" | custom-call | flops 1073741824 | bytes 3145728 | tf_op jit(solution)/shard_map/pallas_call | solution.py:430
  35.6 0.6 %fusion = (f32[8,128]{1,0:T(8,128)}, f32[8,128]{1,0:T(8,128)}) fusion(f32[16,128]{1,0:T(8,128)S(1)} %shard_map.77), kind=kLoop, calls=%fused_computation | loop fusion | bytes 16384 | tf_op jit(solution)/shard_map/slice | solution.py:470
